TPU v7x, 1024 devices: a whole 4x4x32 slice. The times are simulated.
1024 devices in a mesh: wide: 128 (over y, z_lo, core), narrow: 8 (over x, z_hi).
Axes of the slice: x: 4, y: 4, z: 32 (z_hi: 2, z_lo: 16; z = z_hi * 16 + z_lo), core: 2. Of those that a mesh axis runs over, the one named last changes fastest.
Arguments:
- features: bfloat16 [262144, 128], P(('wide', 'narrow')), may hold values from -6 to 6
- w_self: bfloat16 [128, 256], replicated, may hold values from -0.5 to 0.5
- w_neigh: bfloat16 [128, 256], replicated, may hold values from -3 to 3
- cotangent: bfloat16 [262144, 256], P(('wide', 'narrow')), may hold values from -6 to 6
- tile_src: int32 [2048, 20], P(('wide', 'narrow')), may hold values from 0 to 79, as said below
- tile_live: int32 [2048], P(('wide', 'narrow')), may hold values from 2 to 20, as said below
- tile_mask: int32 [2048, 20, 128, 128], P(('wide', 'narrow')), may hold values 0 or 1
Outputs:
- output: bfloat16 [262144, 256], P(('wide', 'narrow'))
- grad_self: float32 [128, 256], replicated
- grad_neigh: float32 [128, 256], replicated
- grad_input: bfloat16 [262144, 128], P(('wide', 'narrow'))
Inputs may be any that keep to these rules, and one draw needn't show every extreme that they name: `tile_src`: the 20 entries of a row are different. Entry s names tile s % 16 of the row block that lies s // 16 - 2 places further along the closed order of row blocks. Slots from tile_live onward are unused whatever their mask holds; some row tile uses all 20 slots.
All inputs are finite; a program needn't handle non-finite values. No bound on the sum of `tile_mask` on one device may be relied on, other than what follows from the above.
Results may differ from a plain program's by a relative error of at most 0.0057.
Values may be sent and summed in bfloat16 or wider, within the bound.
A program may use at most 32 MiB of HBM per device.

v0:
```python
import math

import jax
import jax.numpy as jnp
from jax import lax
from jax.sharding import PartitionSpec as P

REACH = 2


def shifted(value, axis, by):
    devices = lax.axis_size(axis)
    return lax.ppermute(value, axis, [(i, (i + by) % devices) for i in range(devices)])


def fetch_near(source):
    nearby = {0: source}
    for heading in (1, -1):
        for stride in range(1, REACH + 1):
            nearby[heading * stride] = shifted(source, "wide", -heading * stride)
    return jnp.stack([nearby[offset] for offset in range(-REACH, REACH + 1)])


def deliver(partials):
    gathered_sum = partials[REACH]
    for heading in (1, -1):
        for stride in range(1, REACH + 1):
            gathered_sum = gathered_sum + shifted(
                partials[REACH + heading * stride], "wide", heading * stride
            )
    return gathered_sum


def body(features, w_self, w_neigh, cotangent, tile_src, tile_live, tile_mask):
    row_count, width = features.shape
    tile_size = tile_mask.shape[-1]
    slot_count = tile_mask.shape[1]
    dest_tiles = row_count // tile_size
    block_tiles = lax.axis_size("narrow") * dest_tiles
    window_count = (2 * REACH + 1) * block_tiles
    slot_ids = jnp.arange(slot_count, dtype=jnp.int32)
    live_slots = slot_ids[None, :] < tile_live[:, None]
    live_mask = jnp.where(live_slots[:, :, None, None], tile_mask, 0)
    adjacency = live_mask.astype(jnp.bfloat16)
    degree = jnp.sum(live_mask, axis=(1, 3)).astype(jnp.float32).reshape(row_count)
    scaling = 1.0 / (1.0 + degree)
    block = lax.all_gather(features, "narrow", axis=0, tiled=True)
    window = fetch_near(block)
    window_tiles = window.reshape(window_count, tile_size, width)
    picked = window_tiles[tile_src]
    summed = jnp.einsum(
        "dcij,dcjf->dif", adjacency, picked, preferred_element_type=jnp.float32
    ).reshape(row_count, width)
    mean_rows = (summed * scaling[:, None]).astype(jnp.bfloat16)
    preact = jnp.dot(features, w_self, preferred_element_type=jnp.float32) + jnp.dot(
        mean_rows, w_neigh, preferred_element_type=jnp.float32
    )
    output = jax.nn.silu(preact).astype(jnp.bfloat16)
    sigmoid_pre = jax.nn.sigmoid(preact)
    grad_pre = (
        cotangent.astype(jnp.float32) * sigmoid_pre * (1.0 + preact * (1.0 - sigmoid_pre))
    ).astype(jnp.bfloat16)
    rows_first = (((0,), (0,)), ((), ()))
    local_self = lax.dot_general(features, grad_pre, rows_first, preferred_element_type=jnp.float32)
    local_neigh = lax.dot_general(
        mean_rows, grad_pre, rows_first, preferred_element_type=jnp.float32
    )
    grad_self, grad_neigh = lax.psum((local_self, local_neigh), ("wide", "narrow"))
    factor = 1.0 / math.sqrt(row_count * lax.axis_size("wide") * lax.axis_size("narrow"))
    hidden_last = (((1,), (1,)), ((), ()))
    pulled = (
        lax.dot_general(grad_pre, w_neigh, hidden_last, preferred_element_type=jnp.float32)
        * scaling[:, None]
    ).astype(jnp.bfloat16)
    local_term = lax.dot_general(grad_pre, w_self, hidden_last, preferred_element_type=jnp.float32)
    terms = jnp.einsum(
        "dcij,dif->dcjf",
        adjacency,
        pulled.reshape(dest_tiles, tile_size, width),
        preferred_element_type=jnp.float32,
    )
    onehot = (
        tile_src.reshape(-1)[:, None] == jnp.arange(window_count, dtype=jnp.int32)[None, :]
    ).astype(jnp.float32)
    spread = jnp.einsum(
        "cs,cjf->sjf", onehot, terms.reshape(-1, tile_size, width), precision=lax.Precision.HIGHEST
    )
    partials = spread.reshape(2 * REACH + 1, block_tiles * tile_size, width)
    own_rows = lax.psum_scatter(deliver(partials), "narrow", scatter_dimension=0, tiled=True)
    grad_input = (local_term + own_rows).astype(jnp.bfloat16)
    return (output, grad_self * factor, grad_neigh * factor, grad_input)


def solution(mesh):
    return jax.shard_map(
        body,
        mesh=mesh,
        in_specs=(
            P(("wide", "narrow"), None),
            P(),
            P(),
            P(("wide", "narrow"), None),
            P(("wide", "narrow"), None),
            P(("wide", "narrow")),
            P(("wide", "narrow"), None, None, None),
        ),
        out_specs=(P(("wide", "narrow"), None), P(), P(), P(("wide", "narrow"), None)),
        check_vma=False,
    )
```

profile of v0, /device:TPU:1, one launch (start us, length us, event | category | flops | bytes accessed | tf_op | source)
XLA Modules:
  0.0 1177.8 jit_solution(12580519359641121765)
XLA Ops:
  8.1 157.8 %all_gather.3 = bf16[2048,128]{1,0:T(8,128)(2,1)S(1)} all-gather(bf16[256,128]{1,0:T(8,128)(2,1)} %param.7), channel_id=1, replica_groups=mesh['wide'=128,'narrow'=8] {'narrow'}, dimensions={0}, use_global_device_ids=true | all-gather | bytes 589824 | tf_op jit(solution)/shard_map/all_gather | solution.py:47
  165.9 1.9 collective-permute-start
  167.8 14.9 %collective-permute-start.1 = (bf16[2048,128]{1,0:T(8,128)(2,1)S(1)}, bf16[2048,128]{1,0:T(8,128)(2,1)S(1)}, u32[]{:S(2)}, u32[]{:S(2)}) collective-permute-start(bf16[2048,128]{1,0:T(8,128)(2,1)S(1)} %all_gather.3), channel_id=1, source_target_pairs={{0,8},{8,16},{16,24},{24,32},{32,40},{40,48},{48,56},{56,64},{64,7... | collective-permute-start | bytes 1572872 | tf_op jit(solution)/shard_map/ppermute | solution.py:13
  182.7 2.2 collective-permute-start.2
  184.9 21.6 %collective-permute-start.3 = (bf16[2048,128]{1,0:T(8,128)(2,1)S(1)}, bf16[2048,128]{1,0:T(8,128)(2,1)}, u32[]{:S(2)}, u32[]{:S(2)}) collective-permute-start(bf16[2048,128]{1,0:T(8,128)(2,1)S(1)} %all_gather.3), channel_id=1, source_target_pairs={{0,1008},{8,1016},{16,0},{24,8},{32,16},{40,24},{48,32},{56,40},{6... | collective-permute-start | bytes 1572872 | tf_op jit(solution)/shard_map/ppermute | solution.py:13
  208.0 2.1 select_reduce_fusion
  212.9 1.3 collective-permute-done.2
  214.2 1.9 bitcast_dynamic-update-slice_fusion.1
  216.1 2.1 collective-permute-done.3
  218.2 1.9 bitcast_dynamic-update-slice_fusion
  220.1 3.6 gather_fusion
  223.7 1.9 fusion.7
  227.9 4.0 fusion
  232.7 5.8 collective-permute-start.4
  239.8 5.8 collective-permute-start.5
  245.5 1.3 copy.17
  246.9 1.9 collective-permute-start.6
  250.1 19.8 %collective-permute-start.7 = (f32[2048,128]{1,0:T(8,128)}, f32[2048,128]{1,0:T(8,128)}, u32[]{:S(2)}, u32[]{:S(2)}) collective-permute-start(f32[2048,128]{1,0:T(8,128)} %bitcast.21), channel_id=1, source_target_pairs={{0,1008},{8,1016},{16,0},{24,8},{32,16},{40,24},{48,32},{56,40},{6... | collective-permute-start | bytes 3145736 | tf_op jit(solution)/shard_map/ppermute | solution.py:13
  272.2 27.8 %collective-permute-done.5 = f32[2048,128]{1,0:T(8,128)} collective-permute-done((f32[2048,128]{1,0:T(8,128)}, f32[2048,128]{1,0:T(8,128)}, u32[]{:S(2)}, u32[]{:S(2)}) %collective-permute-start.5) | collective-permute-done | bytes 1048608 | tf_op jit(solution)/shard_map/ppermute | solution.py:13
  300.0 6.0 collective-permute-done.6
  306.0 5.5 collective-permute-done.7
  311.4 3.4 fusion.5
  315.0 851.3 %all-reduce.3.cloned.1.call-done = (f32[128,256]{0,1:T(8,128)}, f32[128,256]{0,1:T(8,128)}) async-done(((f32[128,256]{0,1:T(8,128)}, f32[128,256]{0,1:T(8,128)}), (f32[128,256]{0,1:T(8,128)}, f32[128,256]{0,1:T(8,128)})) %all-reduce.3.cloned.1.call-update) | async-done | bytes 262160 | tf_op jit(solution)/shard_map/psum | solution.py:68
  1168.8 1.5 add_convert_fusion
  (47 shorter events, 14.9 us)
Async XLA Ops:
  8.0 217.7 %copy-start = (bf16[128,256]{1,0:T(8,128)(2,1)S(1)}, bf16[128,256]{1,0:T(8,128)(2,1)}, u32[]{:S(2)}) copy-start(bf16[128,256]{1,0:T(8,128)(2,1)} %param.9) | copy-start | bytes 196612
  8.0 202.0 %copy-start.2 = (bf16[256,128]{1,0:T(8,128)(2,1)S(1)}, bf16[256,128]{1,0:T(8,128)(2,1)}, u32[]{:S(2)}) copy-start(bf16[256,128]{1,0:T(8,128)(2,1)} %param.7) | copy-start | bytes 196612
  8.0 202.2 %copy-start.5 = (s32[2,20]{1,0:T(2,128)S(1)}, s32[2,20]{1,0:T(2,128)}, u32[]{:S(2)}) copy-start(s32[2,20]{1,0:T(2,128)} %param.11) | copy-start | bytes 484
  8.0 202.0 %copy-start.3 = (bf16[128,256]{1,0:T(8,128)(2,1)S(1)}, bf16[128,256]{1,0:T(8,128)(2,1)}, u32[]{:S(2)}) copy-start(bf16[128,256]{1,0:T(8,128)(2,1)} %param.8) | copy-start | bytes 196612
  8.0 1158.3 %all-reduce.3.cloned.1.call-start = ((), (), s32[]{:S(2)}) async-start(), calls=%async_computation.2 | async-start | bytes 524288 | tf_op jit(solution)/shard_map/psum | solution.py:68
  165.9 44.5 %collective-permute-start = (bf16[2048,128]{1,0:T(8,128)(2,1)S(1)}, bf16[2048,128]{1,0:T(8,128)(2,1)S(1)}, u32[]{:S(2)}, u32[]{:S(2)}) collective-permute-start(bf16[2048,128]{1,0:T(8,128)(2,1)S(1)} %all_gather.3), channel_id=1, source_target_pairs={{0,16},{8,24},{16,32},{24,40},{32,48},{40,56},{48,64},{56,72},{64,... | collective-permute-start | bytes 1572872 | tf_op jit(solution)/shard_map/ppermute | solution.py:13
  167.8 43.4 %collective-permute-start.1 = (bf16[2048,128]{1,0:T(8,128)(2,1)S(1)}, bf16[2048,128]{1,0:T(8,128)(2,1)S(1)}, u32[]{:S(2)}, u32[]{:S(2)}) collective-permute-start(bf16[2048,128]{1,0:T(8,128)(2,1)S(1)} %all_gather.3), channel_id=1, source_target_pairs={{0,8},{8,16},{16,24},{24,32},{32,40},{40,48},{48,56},{56,64},{64,7... | collective-permute-start | bytes 1572872 | tf_op jit(solution)/shard_map/ppermute | solution.py:13
  182.7 31.5 %collective-permute-start.2 = (bf16[2048,128]{1,0:T(8,128)(2,1)S(1)}, bf16[2048,128]{1,0:T(8,128)(2,1)}, u32[]{:S(2)}, u32[]{:S(2)}) collective-permute-start(bf16[2048,128]{1,0:T(8,128)(2,1)S(1)} %all_gather.3), channel_id=1, source_target_pairs={{0,1016},{8,0},{16,8},{24,16},{32,24},{40,32},{48,40},{56,48},{64,... | collective-permute-start | bytes 1572872 | tf_op jit(solution)/shard_map/ppermute | solution.py:13
  184.9 33.4 %collective-permute-start.3 = (bf16[2048,128]{1,0:T(8,128)(2,1)S(1)}, bf16[2048,128]{1,0:T(8,128)(2,1)}, u32[]{:S(2)}, u32[]{:S(2)}) collective-permute-start(bf16[2048,128]{1,0:T(8,128)(2,1)S(1)} %all_gather.3), channel_id=1, source_target_pairs={{0,1008},{8,1016},{16,0},{24,8},{32,16},{40,24},{48,32},{56,40},{6... | collective-permute-start | bytes 1572872 | tf_op jit(solution)/shard_map/ppermute | solution.py:13
  212.9 10.9 copy-start.1
  223.7 2.0 copy-start.6
  232.7 39.4 %collective-permute-start.4 = (f32[2048,128]{1,0:T(8,128)S(1)}, f32[2048,128]{1,0:T(8,128)}, u32[]{:S(2)}, u32[]{:S(2)}) collective-permute-start(f32[2048,128]{1,0:T(8,128)S(1)} %bitcast.60), channel_id=1, source_target_pairs={{0,8},{8,16},{16,24},{24,32},{32,40},{40,48},{48,56},{56,64},{64,7... | collective-permute-start | bytes 3145736 | tf_op jit(solution)/shard_map/ppermute | solution.py:13
  239.8 60.2 %collective-permute-start.5 = (f32[2048,128]{1,0:T(8,128)}, f32[2048,128]{1,0:T(8,128)}, u32[]{:S(2)}, u32[]{:S(2)}) collective-permute-start(f32[2048,128]{1,0:T(8,128)} %bitcast.19), channel_id=1, source_target_pairs={{0,16},{8,24},{16,32},{24,40},{32,48},{40,56},{48,64},{56,72},{64,... | collective-permute-start | bytes 3145736 | tf_op jit(solution)/shard_map/ppermute | solution.py:13
  246.9 59.1 %collective-permute-start.6 = (f32[2048,128]{1,0:T(8,128)}, f32[2048,128]{1,0:T(8,128)}, u32[]{:S(2)}, u32[]{:S(2)}) collective-permute-start(f32[2048,128]{1,0:T(8,128)} %bitcast.20), channel_id=1, source_target_pairs={{0,1016},{8,0},{16,8},{24,16},{32,24},{40,32},{48,40},{56,48},{64,... | collective-permute-start | bytes 3145736 | tf_op jit(solution)/shard_map/ppermute | solution.py:13
  250.1 61.3 %collective-permute-start.7 = (f32[2048,128]{1,0:T(8,128)}, f32[2048,128]{1,0:T(8,128)}, u32[]{:S(2)}, u32[]{:S(2)}) collective-permute-start(f32[2048,128]{1,0:T(8,128)} %bitcast.21), channel_id=1, source_target_pairs={{0,1008},{8,1016},{16,0},{24,8},{32,16},{40,24},{48,32},{56,40},{6... | collective-permute-start | bytes 3145736 | tf_op jit(solution)/shard_map/ppermute | solution.py:13
  272.1 42.7 %copy-start.4 = (bf16[128,256]{1,0:T(8,128)(2,1)S(1)}, bf16[128,256]{1,0:T(8,128)(2,1)}, u32[]{:S(2)}) copy-start(bf16[128,256]{1,0:T(8,128)(2,1)} %param.8) | copy-start | bytes 196612
  272.1 896.7 %reduce-scatter.2.cloned.1.call-start = ((), (), s32[]{:S(2)}) async-start(), calls=%async_computation.1 | async-start | bytes 1179648 | tf_op jit(solution)/shard_map/reduce_scatter | solution.py:89
Sparse Core Ops, SparseCore 0:
  272.2 894.0 all-reduce.2
Sparse Core Ops, SparseCore 1:
  314.9 195.8 reduce-scatter.1
where the time goes:
time: 1180 us
  waiting for transfers between devices  894 us (76%)
  blocking collectives  158 us (13%)
  starting transfers between devices  73.9 us (6%)
  local copies, waits for them, and re-layouts  16.7 us (1%)
  between operations  15.7 us (1%)
    psum x1, waiting for transfers between devices, body(): lax.psum((local_self, local_neigh), ('wide', 'narrow'))  851 us
    all_gather x1, blocking collectives, body(): block = lax.all_gather(features, 'narrow', axis=0, tiled=True)  158 us
    ppermute x8, starting transfers between devices, shifted(): lax.ppermute(value, axis, [(i, (i + by) % devices) for i in range(devices)])  73.8 us
    ppermute x8, waiting for transfers between devices, shifted(): lax.ppermute(value, axis, [(i, (i + by) % devices) for i in range(devices)])  42.7 us
  transfers between devices with their start and end apart: 10, of which 6 were waited for; matrix products, arithmetic and copies ran while one was open for 2% of the time, Pallas kernels for 0%

commit v1 on v0

v1 whole, which is shorter than its diff:
```python
import functools
import math

import jax
import jax.numpy as jnp
from jax import lax
from jax.experimental import pallas as pl
from jax.experimental.pallas import tpu as pltpu
from jax.sharding import PartitionSpec as P

REACH = 2
WINDOW = 2 * REACH + 1
XS, YS, ZS, CORES = 4, 4, 32, 2
Z_LO = 16
TILE = 128
SHARD = 2 * TILE
BLOCK_TILES = 16
WINDOW_TILES = WINDOW * BLOCK_TILES
SHARDS = WINDOW_TILES // 2
TRANSFERS = 128
GREETINGS = 17
F32 = jnp.float32
BF16 = jnp.bfloat16


def device_of(x, y, z, core):
    return ((y * Z_LO + z % Z_LO) * CORES + core, x * 2 + z // Z_LO)


def kernel(
    slots,
    features_hbm,
    w_self_hbm,
    w_neigh_hbm,
    cotangent_hbm,
    tile_src_hbm,
    tile_live_hbm,
    tile_mask_hbm,
    output,
    grad_self,
    grad_neigh,
    grad_input,
    w_self,
    w_neigh,
    cotangent,
    tile_src,
    tile_live,
    mask_in,
    mask_rows,
    mask_cols,
    slot_vec,
    slot_of,
    adj,
    adj_t,
    win,
    summed,
    degree,
    pre_self,
    mean_rows,
    pulled,
    local_term,
    core_out,
    core_in,
    x_out,
    x_in,
    own_part,
    z_out,
    z_in,
    own_total,
    far_out,
    far_in,
    grads,
    grads_core,
    grads_y,
    grads_x,
    grads_pair,
    grads_near,
    grads_far,
    grads_all,
    send_sem,
    recv_sem,
    load_sem,
    slot_sem,
):
    wide, narrow = lax.axis_index("wide"), lax.axis_index("narrow")
    core = wide % 2
    z_lo = (wide // 2) % Z_LO
    y = wide // (2 * Z_LO)
    x = narrow // 2
    h = narrow % 2
    z = h * Z_LO + z_lo

    other_core = device_of(x, y, z, 1 - core)
    xs = [(x + step) % XS for step in (1, 3, 2)]
    ys = [(y + step) % YS for step in (1, 3, 2)]
    from_xs = [xs[1], xs[0], xs[2]]
    x_devices = [device_of(to, y, z, core) for to in xs]
    y_devices = [device_of(x, to, z, core) for to in ys]
    far = device_of(x, y, (z + 16) % ZS, core)
    prev_y = jnp.where(z_lo == 0, (y + YS - 1) % YS, y)
    next_y = jnp.where(z_lo == Z_LO - 1, (y + 1) % YS, y)
    prev_z, next_z = (z + ZS - 1) % ZS, (z + 1) % ZS
    prev = device_of(x, prev_y, prev_z, core)
    next_ = device_of(x, next_y, next_z, core)
    pair_z = z + 1 - 2 * (z % 2)
    pair = device_of(x, y, pair_z, core)
    near_slot = (z // 2) % 4
    near_devices = [
        device_of(x, y, (z // 8) * 8 + ((near_slot + step) % 4) * 2 + z % 2, core) for step in (1, 3, 2)
    ]
    far_slot = z // 8
    far_devices = [device_of(x, y, ((far_slot + step) % 4) * 8 + z % 8, core) for step in (1, 3, 2)]
    h_prev, h_next = prev_z // Z_LO, next_z // Z_LO

    barrier = pltpu.get_barrier_semaphore()
    greeted = [other_core, *x_devices, *y_devices, far, prev, next_, pair, *near_devices, *far_devices]
    for device in greeted:
        pl.semaphore_signal(barrier, inc=1, device_id=device, device_id_type=pl.DeviceIdType.MESH)

    sent = []

    def send(source, target, device):
        number = len(sent)
        copy = pltpu.make_async_remote_copy(
            src_ref=source,
            dst_ref=target,
            send_sem=send_sem.at[number],
            recv_sem=recv_sem.at[number],
            device_id=device,
            device_id_type=pl.DeviceIdType.MESH,
        )
        copy.start()
        sent.append(copy)
        return copy

    loads = [
        pltpu.make_async_copy(source, target, load_sem.at[number])
        for number, (source, target) in enumerate(
            (
                (tile_src_hbm, tile_src),
                (tile_live_hbm, tile_live),
                (features_hbm, win.at[2, x, h]),
                (w_self_hbm, w_self),
                (tile_mask_hbm, mask_in),
                (w_neigh_hbm, w_neigh),
                (cotangent_hbm, cotangent),
            )
        )
    ]
    for load in loads:
        load.start()
    load_src, load_live, load_features, load_self, load_mask, load_neigh, load_cotangent = loads

    load_src.wait()
    load_live.wait()
    window_tile = lax.broadcasted_iota(jnp.int32, (8, TILE), 1)
    for d in range(2):

        def find(c, found, d=d):
            source = jnp.where(c < tile_live[d], tile_src[d, c], -1)
            return jnp.where(window_tile == source, c, found)

        slot_vec[d * 8 : d * 8 + 8, :] = lax.fori_loop(0, slots, find, jnp.full((8, TILE), slots, jnp.int32))
    load_slots = pltpu.make_async_copy(slot_vec, slot_of, slot_sem)
    load_slots.start()

    load_features.wait()
    load_self.wait()
    pre_self[...] = jnp.dot(win[2, x, h], w_self[...], preferred_element_type=F32)
    core_in[0, 2 * core] = jnp.zeros((XS, SHARD, TILE), BF16)
    core_in[1, 2 * core] = jnp.zeros((XS, SHARD, TILE), BF16)
    for d in range(2):
        mask_rows[d * (slots + 1) + slots] = jnp.zeros((TILE, TILE), BF16)
        mask_cols[d * (slots + 1) + slots] = jnp.zeros((TILE, TILE), BF16)

    load_mask.wait()
    for d in range(2):

        @pl.loop(0, slots)
        def _(c, d=d):
            tile = mask_in[d, c].astype(F32)
            mask_rows[d * (slots + 1) + c] = tile.astype(BF16)
            mask_cols[d * (slots + 1) + c] = tile.T.astype(BF16)

    pl.semaphore_wait(barrier, GREETINGS)

    side_p = 4 - 4 * core
    side_h = jnp.where(core == 0, h_next, h_prev)

    def spread(hi, first):
        own = win.at[2, x, hi]
        to_far = send(own, own, far) if first else None
        to_next = send(own, win.at[0, x, hi], next_)
        to_prev = send(own, win.at[4, x, hi], prev)
        over_x = [send(own, own, device) for device in x_devices]
        to_core = send(own, win.at[1 + 2 * core, x, hi], other_core)
        return to_far, to_next, to_prev, over_x, to_core

    def spread_sides(flip, to_next, to_prev):
        hi_prev, hi_next = (h_prev, h_next) if flip == 0 else (1 - h_prev, 1 - h_next)
        side = side_h if flip == 0 else 1 - side_h
        to_next.wait_recv()
        from_prev = win.at[0, x, hi_prev]
        over_prev = [send(from_prev, from_prev, device) for device in x_devices]
        to_prev.wait_recv()
        from_next = win.at[4, x, hi_next]
        over_next = [send(from_next, from_next, device) for device in x_devices]
        to_core = send(win.at[side_p, x, side], win.at[3 - 2 * core, x, side], other_core)
        return over_prev, over_next, to_core

    def spread_cores(flip, over_x, over_prev, over_next):
        hi = h if flip == 0 else 1 - h
        side = side_h if flip == 0 else 1 - side_h
        copies = []
        for j in range(3):
            over_x[j].wait_recv()
            copies.append(send(win.at[2, from_xs[j], hi], win.at[1 + 2 * core, from_xs[j], hi], other_core))
        for j in range(3):
            over_prev[j].wait_recv()
            over_next[j].wait_recv()
            copies.append(
                send(
                    win.at[side_p, from_xs[j], side], win.at[3 - 2 * core, from_xs[j], side], other_core
                )
            )
        return copies

    def sides(flip):
        parts = [h_prev, jnp.where(core == 0, h_prev, h), h, jnp.where(core == 0, h, h_next), h_next]
        return parts if flip == 0 else [1 - part for part in parts]

    to_far, to_next, to_prev, over_x, to_core = spread(h, True)

    load_slots.wait()
    degree[...] = jnp.zeros((SHARD, TILE), F32)

    @pl.loop(0, SHARDS)
    def _(s):
        for t in range(2):
            for d in range(2):
                index = d * (slots + 1) + jnp.clip(slot_of[8 * d, 2 * s + t], 0, slots)
                adj[s, pl.ds(d * TILE, TILE), pl.ds(t * TILE, TILE)] = mask_rows[index]
                adj_t[s, pl.ds(t * TILE, TILE), pl.ds(d * TILE, TILE)] = mask_cols[index]
        degree[...] += jnp.dot(adj[s], jnp.ones((SHARD, TILE), BF16), preferred_element_type=F32)

    over_prev, over_next, side_core = spread_sides(0, to_next, to_prev)
    cores_0 = spread_cores(0, over_x, over_prev, over_next)

    summed[...] = jnp.zeros((SHARD, TILE), F32)

    def aggregate(blocks, parts):
        for p in blocks:

            @pl.loop(0, XS)
            def _(xo, p=p):
                summed[...] += jnp.dot(
                    adj[(p * XS + xo) * 2 + parts[p]], win[p, xo, parts[p]], preferred_element_type=F32
                )

    parts_0, parts_1 = sides(0), sides(1)
    aggregate((0, 2, 4), parts_0)

    to_far.wait_recv()
    _, to_next_1, to_prev_1, over_x_1, to_core_1 = spread(1 - h, False)
    to_core.wait_recv()
    side_core.wait_recv()
    for copy in cores_0:
        copy.wait_recv()
    aggregate((1, 3), parts_0)
    over_prev_1, over_next_1, side_core_1 = spread_sides(1, to_next_1, to_prev_1)
    cores_1 = spread_cores(1, over_x_1, over_prev_1, over_next_1)
    aggregate((0, 2, 4), parts_1)
    to_core_1.wait_recv()
    side_core_1.wait_recv()
    for copy in cores_1:
        copy.wait_recv()
    aggregate((1, 3), parts_1)

    load_neigh.wait()
    load_cotangent.wait()
    scaling = 1.0 / (1.0 + degree[...])
    mean_rows[...] = (summed[...] * scaling).astype(BF16)
    preact = pre_self[...] + jnp.dot(mean_rows[...], w_neigh[...], preferred_element_type=F32)
    sigmoid = jax.nn.sigmoid(preact)
    output[...] = (preact * sigmoid).astype(BF16)
    grad_pre = (cotangent[...].astype(F32) * sigmoid * (1.0 + preact * (1.0 - sigmoid))).astype(BF16)
    rows_first = (((0,), (0,)), ((), ()))
    hidden_last = (((1,), (1,)), ((), ()))
    grads[0] = lax.dot_general(win[2, x, h], grad_pre, rows_first, preferred_element_type=F32)
    grads[1] = lax.dot_general(mean_rows[...], grad_pre, rows_first, preferred_element_type=F32)
    core_grads = send(grads.at[1 - core], grads_core, other_core)
    pulled[...] = (
        lax.dot_general(grad_pre, w_neigh[...], hidden_last, preferred_element_type=F32) * scaling
    ).astype(BF16)
    local_term[...] = lax.dot_general(grad_pre, w_self[...], hidden_last, preferred_element_type=F32)

    def to_cores(phase, parts):
        copies = []
        for i in range(2):
            p = 2 * i + 1

            @pl.loop(0, XS)
            def _(xo, i=i, p=p):
                core_out[phase, i, xo] = jnp.dot(
                    adj_t[(p * XS + xo) * 2 + parts[p]], pulled[...], preferred_element_type=F32
                ).astype(BF16)

            copies.append(send(core_out.at[phase, i], core_in.at[phase, i + core], other_core))
        return copies

    def over_x_back(phase, parts, blocks):
        copies = []
        for q in blocks:
            p = 2 * q

            @pl.loop(0, 3)
            def _(j, q=q, p=p):
                step = jnp.where(j == 0, 1, jnp.where(j == 1, 3, 2))
                xo = (x + step) % XS
                x_out[phase, q, j] = (
                    jnp.dot(
                        adj_t[(p * XS + xo) * 2 + parts[p]], pulled[...], preferred_element_type=F32
                    )
                    + core_in[phase, q, xo].astype(F32)
                ).astype(BF16)

            for j in range(3):
                copies.append(send(x_out.at[phase, q, j], x_in.at[phase, q, j], x_devices[j]))
        for q in blocks:
            p = 2 * q
            own_part[phase, q] = jnp.dot(
                adj_t[(p * XS + x) * 2 + parts[p]], pulled[...], preferred_element_type=F32
            ) + core_in[phase, q, x].astype(F32)
        return copies

    def x_sum(phase, q):
        total = own_part[phase, q]
        for j in range(3):
            total = total + x_in[phase, q, j].astype(F32)
        return total

    def to_sides(phase, copies):
        for copy in copies:
            copy.wait_recv()
        z_out[phase, 0] = x_sum(phase, 0).astype(BF16)
        to_prev = send(z_out.at[phase, 0], z_in.at[phase, 1], prev)
        z_out[phase, 1] = x_sum(phase, 2).astype(BF16)
        to_next = send(z_out.at[phase, 1], z_in.at[phase, 0], next_)
        return to_prev, to_next

    cores_back_1 = to_cores(1, parts_1)
    cores_back_0 = to_cores(0, parts_0)
    core_grads.wait_recv()
    grads[core] = grads[core] + grads_core[...]
    y_rows = TILE // YS
    x_rows = y_rows // XS
    y_grads = [
        send(grads.at[core, pl.ds(ys[j] * y_rows, y_rows)], grads_y.at[j], y_devices[j]) for j in range(3)
    ]
    for copy in cores_back_1:
        copy.wait_recv()
    x_sides_1 = over_x_back(1, parts_1, (0, 2))
    x_own_1 = over_x_back(1, parts_1, (1,))
    for copy in y_grads:
        copy.wait_recv()
    own_rows = pl.ds(y * y_rows, y_rows)
    grads_all[0, :y_rows] = grads[core, own_rows] + grads_y[0] + grads_y[1] + grads_y[2]
    x_grads = [
        send(grads_all.at[0, pl.ds(xs[j] * x_rows, x_rows)], grads_x.at[j], x_devices[j]) for j in range(3)
    ]
    for copy in cores_back_0:
        copy.wait_recv()
    x_sides_0 = over_x_back(0, parts_0, (0, 2))
    x_own_0 = over_x_back(0, parts_0, (1,))
    for copy in x_grads:
        copy.wait_recv()
    part = grads_all[0, pl.ds(x * x_rows, x_rows)] + grads_x[0] + grads_x[1] + grads_x[2]
    grads_pair[0] = part[:, :TILE]
    grads_pair[1] = part[:, TILE:]
    parity = z % 2
    pair_grads = send(grads_pair.at[1 - parity], grads_pair.at[2], pair)
    pair_grads.wait_recv()
    grads_near[near_slot] = grads_pair[parity] + grads_pair[2]
    near_grads = [send(grads_near.at[near_slot], grads_near.at[near_slot], device) for device in near_devices]
    sides_1 = to_sides(1, x_sides_1)
    for copy in near_grads:
        copy.wait_recv()
    grads_far[far_slot] = grads_near[0] + grads_near[1] + grads_near[2] + grads_near[3]
    far_grads = [send(grads_far.at[far_slot], grads_far.at[far_slot], device) for device in far_devices]
    for copy in (*x_own_1, *sides_1):
        copy.wait_recv()
    far_out[...] = (x_sum(1, 1) + z_in[1, 0].astype(F32) + z_in[1, 1].astype(F32)).astype(BF16)
    to_far_back = send(far_out, far_in, far)
    sides_0 = to_sides(0, x_sides_0)
    for copy in (*x_own_0, *sides_0):
        copy.wait_recv()
    own_total[...] = (
        local_term[...] + x_sum(0, 1) + z_in[0, 0].astype(F32) + z_in[0, 1].astype(F32)
    )
    for copy in far_grads:
        copy.wait_recv()
    factor = 1.0 / math.sqrt(SHARD * lax.axis_size("wide") * lax.axis_size("narrow"))
    total = (grads_far[0] + grads_far[1] + grads_far[2] + grads_far[3]) * factor
    row = y * y_rows + x * x_rows
    piece = grads_all.at[1 + core, pl.ds(row, x_rows), pl.ds(pl.multiple_of(parity * TILE, TILE), TILE)]
    piece[...] = total
    send(piece, piece, pair).wait_recv()
    piece = grads_all.at[1 + core, pl.ds(row, x_rows)]
    for copy in [send(piece, piece, device) for device in x_devices]:
        copy.wait_recv()
    piece = grads_all.at[1 + core, pl.ds(y * y_rows, y_rows)]
    for copy in [send(piece, piece, device) for device in y_devices]:
        copy.wait_recv()
    piece = grads_all.at[1 + core]
    send(piece, piece, other_core).wait_recv()
    grad_self[...] = grads_all[1]
    grad_neigh[...] = grads_all[2]
    to_far_back.wait_recv()
    grad_input[...] = (own_total[...] + far_in[...].astype(F32)).astype(BF16)
    for copy in sent:
        copy.wait_send()


def body(features, w_self, w_neigh, cotangent, tile_src, tile_live, tile_mask):
    rows, width = features.shape
    hidden = w_self.shape[1]
    slots = tile_src.shape[1]
    vmem = pl.BlockSpec(memory_space=pltpu.VMEM)
    hbm = pl.BlockSpec(memory_space=pl.ANY)
    return pl.pallas_call(
        functools.partial(kernel, slots),
        out_shape=(
            jax.ShapeDtypeStruct((rows, hidden), BF16),
            jax.ShapeDtypeStruct((width, hidden), F32),
            jax.ShapeDtypeStruct((width, hidden), F32),
            jax.ShapeDtypeStruct((rows, width), BF16),
        ),
        in_specs=[hbm] * 7,
        out_specs=[vmem] * 4,
        scratch_shapes=[
            pltpu.VMEM((width, hidden), BF16),
            pltpu.VMEM((width, hidden), BF16),
            pltpu.VMEM((rows, hidden), BF16),
            pltpu.SMEM(tile_src.shape, jnp.int32),
            pltpu.SMEM(tile_live.shape, jnp.int32),
            pltpu.VMEM((2, slots, TILE, TILE), jnp.int32),
            pltpu.VMEM((2 * (slots + 1), TILE, TILE), BF16),
            pltpu.VMEM((2 * (slots + 1), TILE, TILE), BF16),
            pltpu.VMEM((16, TILE), jnp.int32),
            pltpu.SMEM((16, TILE), jnp.int32),
            pltpu.VMEM((SHARDS, SHARD, SHARD), BF16),
            pltpu.VMEM((SHARDS, SHARD, SHARD), BF16),
            pltpu.VMEM((WINDOW, XS, 2, SHARD, TILE), BF16),
            pltpu.VMEM((SHARD, TILE), F32),
            pltpu.VMEM((SHARD, TILE), F32),
            pltpu.VMEM((SHARD, hidden), F32),
            pltpu.VMEM((SHARD, TILE), BF16),
            pltpu.VMEM((SHARD, TILE), BF16),
            pltpu.VMEM((SHARD, TILE), F32),
            pltpu.VMEM((2, 2, XS, SHARD, TILE), BF16),
            pltpu.VMEM((2, 3, XS, SHARD, TILE), BF16),
            pltpu.VMEM((2, 3, 3, SHARD, TILE), BF16),
            pltpu.VMEM((2, 3, 3, SHARD, TILE), BF16),
            pltpu.VMEM((2, 3, SHARD, TILE), F32),
            pltpu.VMEM((2, 2, SHARD, TILE), BF16),
            pltpu.VMEM((2, 2, SHARD, TILE), BF16),
            pltpu.VMEM((SHARD, TILE), F32),
            pltpu.VMEM((SHARD, TILE), BF16),
            pltpu.VMEM((SHARD, TILE), BF16),
            pltpu.VMEM((2, width, hidden), F32),
            pltpu.VMEM((width, hidden), F32),
            pltpu.VMEM((3, width // YS, hidden), F32),
            pltpu.VMEM((3, width // YS // XS, hidden), F32),
            pltpu.VMEM((3, width // YS // XS, TILE), F32),
            pltpu.VMEM((4, width // YS // XS, TILE), F32),
            pltpu.VMEM((4, width // YS // XS, TILE), F32),
            pltpu.VMEM((3, width, hidden), F32),
            pltpu.SemaphoreType.DMA((TRANSFERS,)),
            pltpu.SemaphoreType.DMA((TRANSFERS,)),
            pltpu.SemaphoreType.DMA((7,)),
            pltpu.SemaphoreType.DMA,
        ],
        compiler_params=pltpu.CompilerParams(
            collective_id=1, has_side_effects=True, vmem_limit_bytes=62 * 1024 * 1024
        ),
    )(features, w_self, w_neigh, cotangent, tile_src, tile_live, tile_mask)


def solution(mesh):
    return jax.shard_map(
        body,
        mesh=mesh,
        in_specs=(
            P(("wide", "narrow"), None),
            P(),
            P(),
            P(("wide", "narrow"), None),
            P(("wide", "narrow"), None),
            P(("wide", "narrow")),
            P(("wide", "narrow"), None, None, None),
        ),
        out_specs=(P(("wide", "narrow"), None), P(), P(), P(("wide", "narrow"), None)),
        check_vma=False,
    )
```

time: 1180 us -> 127 us (0.11)
  waiting for transfers between devices: 894 us -> 0 us
  blocking collectives: 158 us -> 0 us
  Pallas kernels: 0 us -> 120 us
  starting transfers between devices: 73.9 us -> 0 us
  between operations: 15.7 us -> 0.64 us
    psum x1 -> x0, waiting for transfers between devices: 851 us -> none  [body(): lax.psum((local_self, local_neigh), ('wide', 'narrow'))]
    all_gather x1 -> x0, blocking collectives: 158 us -> none  [body(): block = lax.all_gather(features, 'narrow', axis=0, tiled=True)]
    pallas_call x0 -> x1, Pallas kernels: none -> 120 us  [body(): pl.pallas_call(functools.partial(kernel, slots), out_shape=(jax.ShapeDtyp...]
    ppermute x8 -> x0, starting transfers between devices: 73.8 us -> none  [shifted(): lax.ppermute(value, axis, [(i, (i + by) % devices) for i in range(devices)])]
    ppermute x8 -> x0, waiting for transfers between devices: 42.7 us -> none  [shifted(): lax.ppermute(value, axis, [(i, (i + by) % devices) for i in range(devices)])]
  transfers between devices with their start and end apart: 10 -> 0, of which waited for: 6 -> 0; matrix products, arithmetic and copies ran while one was open for 2% -> 0% of each run, Pallas kernels for 0% -> 0%
where the time goes in v1:
time: 127 us
  Pallas kernels  120 us (94%)
  local copies, waits for them, and re-layouts  6.17 us (5%)
    pallas_call x1, Pallas kernels, body(): pl.pallas_call(functools.partial(kernel, slots), out_shape=(jax.ShapeDtyp...  120 us
    unnamed x4, local copies, waits for them, and re-layouts  6.17 us

profile of v1, /device:TPU:1, one launch (start us, length us, event | category | flops | bytes accessed | tf_op | source)
XLA Modules:
  0.0 126.7 jit_solution(4879023911204040704)
XLA Ops:
  0.6 119.8 %shard_map.102 = (bf16[256,256]{1,0:T(8,128)(2,1)}, f32[128,256]{1,0:T(8,128)}, f32[128,256]{1,0:T(8,128)}, bf16[256,128]{1,0:T(8,128)(2,1)}) custom-call(bf16[256,128]{1,0:T(8,128)(2,1)} %features_hbm.1, bf16[128,256]{1,0:T(8,128)(2,1)} %w_self_hbm.1, bf16[128,256]{1,0:T(8,128)(2,1)} %w_neigh_hbm.1, bf16[256,256]{1,0:T(8,128)(2,1)} %cotangent_hbm.1, ...), custom_call_target="tpu_custom_call" | custom-call | tf_op jit(solution)/shard_map/pallas_call | solution.py:430
  120.5 1.6 %copy.15 = bf16[256,256]{1,0:T(8,128)(2,1)} copy(bf16[256,256]{1,0:T(8,128)(2,1)} %get-tuple-element.8) | data formatting | bytes 262144
  122.0 1.6 %copy.16 = f32[128,256]{1,0:T(8,128)} copy(f32[128,256]{1,0:T(8,128)} %get-tuple-element.9) | data formatting | bytes 262144
  123.6 1.6 %copy.17 = f32[128,256]{1,0:T(8,128)} copy(f32[128,256]{1,0:T(8,128)} %get-tuple-element.10) | data formatting | bytes 262144
  125.2 1.5 %copy.18 = bf16[256,128]{1,0:T(8,128)(2,1)} copy(bf16[256,128]{1,0:T(8,128)(2,1)} %get-tuple-element.11) | data formatting | bytes 131072

commit v2 on v1

v2 whole, which is shorter than its diff:
```python
import functools
import math

import jax
import jax.numpy as jnp
from jax import lax
from jax.experimental import pallas as pl
from jax.experimental.pallas import tpu as pltpu
from jax.sharding import PartitionSpec as P

REACH = 2
WINDOW = 2 * REACH + 1
XS, YS, ZS, CORES = 4, 4, 32, 2
Z_LO = 16
TILE = 128
SHARD = 2 * TILE
BLOCK_TILES = 16
WINDOW_TILES = WINDOW * BLOCK_TILES
SHARDS = WINDOW_TILES // 2
PLANE = XS * YS
NEAR, FAR = 8, 4
TRANSFERS = 192
F32 = jnp.float32
BF16 = jnp.bfloat16


def device_of(x, y, z, core):
    return ((y * Z_LO + z % Z_LO) * CORES + core, x * 2 + z // Z_LO)


def kernel(
    slots,
    features_hbm,
    w_self_hbm,
    w_neigh_hbm,
    cotangent_hbm,
    tile_src_hbm,
    tile_live_hbm,
    tile_mask_hbm,
    output,
    grad_self,
    grad_neigh,
    grad_input,
    w_self,
    w_neigh,
    cotangent,
    tile_src,
    tile_live,
    mask_in,
    mask_rows,
    mask_cols,
    slot_vec,
    slot_of,
    adj,
    adj_t,
    win,
    summed,
    degree,
    pre_self,
    mean_rows,
    pulled,
    local_term,
    core_out,
    core_in,
    x_out,
    x_in,
    own_part,
    zx_out,
    zx_in,
    z_out,
    z_in,
    own_total,
    far_out,
    far_in,
    grads,
    grads_core,
    grads_plane,
    grads_near,
    grads_far,
    grads_all,
    send_sem,
    recv_sem,
    load_sem,
    slot_sem,
):
    wide, narrow = lax.axis_index("wide"), lax.axis_index("narrow")
    core = wide % 2
    z_lo = (wide // 2) % Z_LO
    y = wide // (2 * Z_LO)
    x = narrow // 2
    h = narrow % 2
    z = h * Z_LO + z_lo

    other_core = device_of(x, y, z, 1 - core)
    xs = [(x + step) % XS for step in (1, 3, 2)]
    from_xs = [xs[1], xs[0], xs[2]]
    x_devices = [device_of(to, y, z, core) for to in xs]
    far = device_of(x, y, (z + 16) % ZS, core)
    prev_y = jnp.where(z_lo == 0, (y + YS - 1) % YS, y)
    next_y = jnp.where(z_lo == Z_LO - 1, (y + 1) % YS, y)
    prev_z, next_z = (z + ZS - 1) % ZS, (z + 1) % ZS
    prev = device_of(x, prev_y, prev_z, core)
    next_ = device_of(x, next_y, next_z, core)
    place = y * XS + x
    places = [(place + step) % PLANE for step in range(1, PLANE)]
    plane_devices = [device_of(to % XS, to // XS, z, core) for to in places]
    near_slot, far_slot = z % NEAR, z // NEAR
    near_devices = [
        device_of(x, y, far_slot * NEAR + (near_slot + step) % NEAR, core) for step in range(1, NEAR)
    ]
    far_devices = [
        device_of(x, y, ((far_slot + step) % FAR) * NEAR + near_slot, core) for step in range(1, FAR)
    ]
    h_prev, h_next = prev_z // Z_LO, next_z // Z_LO

    barrier = pltpu.get_barrier_semaphore()
    greeted = [other_core, *plane_devices, prev, next_, *near_devices, *far_devices]
    for device in greeted:
        pl.semaphore_signal(barrier, inc=1, device_id=device, device_id_type=pl.DeviceIdType.MESH)

    sent = []

    def send(source, target, device):
        number = len(sent)
        copy = pltpu.make_async_remote_copy(
            src_ref=source,
            dst_ref=target,
            send_sem=send_sem.at[number],
            recv_sem=recv_sem.at[number],
            device_id=device,
            device_id_type=pl.DeviceIdType.MESH,
        )
        copy.start()
        sent.append(copy)
        return copy

    loads = [
        pltpu.make_async_copy(source, target, load_sem.at[number])
        for number, (source, target) in enumerate(
            (
                (tile_src_hbm, tile_src),
                (tile_live_hbm, tile_live),
                (features_hbm, win.at[2, x, h]),
                (w_self_hbm, w_self),
                (tile_mask_hbm, mask_in),
                (w_neigh_hbm, w_neigh),
                (cotangent_hbm, cotangent),
            )
        )
    ]
    for load in loads:
        load.start()
    load_src, load_live, load_features, load_self, load_mask, load_neigh, load_cotangent = loads

    load_src.wait()
    load_live.wait()
    window_tile = lax.broadcasted_iota(jnp.int32, (8, TILE), 1)
    for d in range(2):

        def find(c, found, d=d):
            source = jnp.where(c < tile_live[d], tile_src[d, c], -1)
            return jnp.where(window_tile == source, c, found)

        slot_vec[d * 8 : d * 8 + 8, :] = lax.fori_loop(0, slots, find, jnp.full((8, TILE), slots, jnp.int32))
    load_slots = pltpu.make_async_copy(slot_vec, slot_of, slot_sem)
    load_slots.start()

    load_features.wait()
    load_self.wait()
    pre_self[...] = jnp.dot(win[2, x, h], w_self[...], preferred_element_type=F32)
    core_in[0, 2 * core] = jnp.zeros((XS, SHARD, TILE), BF16)
    core_in[1, 2 * core] = jnp.zeros((XS, SHARD, TILE), BF16)
    for d in range(2):
        mask_rows[d * (slots + 1) + slots] = jnp.zeros((TILE, TILE), BF16)
        mask_cols[d * (slots + 1) + slots] = jnp.zeros((TILE, TILE), BF16)

    load_mask.wait()
    degree[...] = jnp.zeros((SHARD, TILE), F32)
    for d in range(2):

        @pl.loop(0, slots)
        def _(c, d=d):
            used = jnp.where(c < tile_live[d], 1, 0)
            degree[pl.ds(d * TILE, TILE)] += (mask_in[d, c] * used).astype(F32)
            tile = mask_in[d, c].astype(F32)
            mask_rows[d * (slots + 1) + c] = tile.astype(BF16)
            mask_cols[d * (slots + 1) + c] = tile.T.astype(BF16)

    degree[...] = jnp.dot(degree[...].astype(BF16), jnp.ones((TILE, TILE), BF16), preferred_element_type=F32)

    pl.semaphore_wait(barrier, len(greeted))

    side_p = 4 - 4 * core
    side_h = jnp.where(core == 0, h_next, h_prev)
    shard = pl.ds(0, SHARD)
    tiles = [pl.ds(t * TILE, TILE) for t in range(2)]

    def spread(flip, rows):
        hi = h if flip == 0 else 1 - h
        own = win.at[2, x, hi, rows]
        to_next = send(own, win.at[0, x, hi, rows], next_)
        to_prev = send(own, win.at[4, x, hi, rows], prev)
        over_x = [send(own, own, x_devices[j]) for j in (2, 0, 1)]
        over_x = [over_x[1], over_x[2], over_x[0]]
        to_core = send(own, win.at[1 + 2 * core, x, hi, rows], other_core)
        return to_next, to_prev, over_x, to_core

    def spread_sides(flip, rows, to_next, to_prev):
        hi_prev, hi_next = (h_prev, h_next) if flip == 0 else (1 - h_prev, 1 - h_next)
        side = side_h if flip == 0 else 1 - side_h
        to_next.wait_recv()
        from_prev = win.at[0, x, hi_prev, rows]
        over_prev = [send(from_prev, from_prev, device) for device in x_devices[:2]]
        to_prev.wait_recv()
        from_next = win.at[4, x, hi_next, rows]
        over_next = [send(from_next, from_next, device) for device in x_devices[:2]]
        to_core = send(win.at[side_p, x, side, rows], win.at[3 - 2 * core, x, side, rows], other_core)
        return over_prev, over_next, to_core

    def spread_cores(flip, rows, over_x, over_prev, over_next):
        hi = h if flip == 0 else 1 - h
        side = side_h if flip == 0 else 1 - side_h

        def side_to_core(xo):
            return send(win.at[side_p, xo, side, rows], win.at[3 - 2 * core, xo, side, rows], other_core)

        over_x[2].wait_recv()
        xo = from_xs[2]
        hops = [
            send(win.at[2, xo, hi, rows], win.at[0, xo, hi, rows], next_),
            send(win.at[2, xo, hi, rows], win.at[4, xo, hi, rows], prev),
        ]
        copies = []
        for j in (2, 0, 1):
            if j != 2:
                over_x[j].wait_recv()
            copies.append(
                send(
                    win.at[2, from_xs[j], hi, rows], win.at[1 + 2 * core, from_xs[j], hi, rows], other_core
                )
            )
        for j in range(2):
            over_prev[j].wait_recv()
            over_next[j].wait_recv()
            copies.append(side_to_core(from_xs[j]))
        for copy in hops:
            copy.wait_recv()
        copies.append(side_to_core(xo))
        return copies

    def sides(flip):
        parts = [h_prev, jnp.where(core == 0, h_prev, h), h, jnp.where(core == 0, h, h_next), h_next]
        return parts if flip == 0 else [1 - part for part in parts]

    to_far = [send(win.at[2, x, h, rows], win.at[2, x, h, rows], far) for rows in tiles]
    to_next, to_prev, over_x, to_core = spread(0, shard)

    load_slots.wait()

    @pl.loop(0, SHARDS)
    def _(s):
        for t in range(2):
            for d in range(2):
                index = d * (slots + 1) + jnp.clip(slot_of[8 * d, 2 * s + t], 0, slots)
                adj[s, pl.ds(d * TILE, TILE), pl.ds(t * TILE, TILE)] = mask_rows[index]
                adj_t[s, pl.ds(t * TILE, TILE), pl.ds(d * TILE, TILE)] = mask_cols[index]

    over_prev, over_next, side_core = spread_sides(0, shard, to_next, to_prev)
    cores_0 = spread_cores(0, shard, over_x, over_prev, over_next)

    summed[...] = jnp.zeros((SHARD, TILE), F32)

    def aggregate(blocks, parts):
        total = summed[...]
        for p in blocks:
            for xo in range(XS):
                total = total + jnp.dot(
                    adj[(p * XS + xo) * 2 + parts[p]], win[p, xo, parts[p]], preferred_element_type=F32
                )
        summed[...] = total

    parts_0, parts_1 = sides(0), sides(1)
    aggregate((0, 2, 4), parts_0)

    to_core.wait_recv()
    side_core.wait_recv()
    for copy in cores_0:
        copy.wait_recv()
    aggregate((1, 3), parts_0)

    to_far[0].wait_recv()
    to_next_0, to_prev_0, over_x_0, to_core_0 = spread(1, tiles[0])
    over_prev_0, over_next_0, side_core_0 = spread_sides(1, tiles[0], to_next_0, to_prev_0)
    to_far[1].wait_recv()
    to_next_1, to_prev_1, over_x_1, to_core_1 = spread(1, tiles[1])
    cores_1 = spread_cores(1, tiles[0], over_x_0, over_prev_0, over_next_0)
    over_prev_1, over_next_1, side_core_1 = spread_sides(1, tiles[1], to_next_1, to_prev_1)
    cores_1 += spread_cores(1, tiles[1], over_x_1, over_prev_1, over_next_1)
    aggregate((0, 2, 4), parts_1)
    for copy in (to_core_0, side_core_0, to_core_1, side_core_1, *cores_1):
        copy.wait_recv()
    aggregate((1, 3), parts_1)

    load_neigh.wait()
    load_cotangent.wait()
    scaling = 1.0 / (1.0 + degree[...])
    mean_rows[...] = (summed[...] * scaling).astype(BF16)
    preact = pre_self[...] + jnp.dot(mean_rows[...], w_neigh[...], preferred_element_type=F32)
    sigmoid = jax.nn.sigmoid(preact)
    output[...] = (preact * sigmoid).astype(BF16)
    grad_pre = (cotangent[...].astype(F32) * sigmoid * (1.0 + preact * (1.0 - sigmoid))).astype(BF16)
    rows_first = (((0,), (0,)), ((), ()))
    hidden_last = (((1,), (1,)), ((), ()))
    grads[0] = lax.dot_general(win[2, x, h], grad_pre, rows_first, preferred_element_type=F32)
    grads[1] = lax.dot_general(mean_rows[...], grad_pre, rows_first, preferred_element_type=F32)
    core_grads = send(grads.at[1 - core], grads_core, other_core)
    pulled[...] = (
        lax.dot_general(grad_pre, w_neigh[...], hidden_last, preferred_element_type=F32) * scaling
    ).astype(BF16)
    local_term[...] = lax.dot_general(grad_pre, w_self[...], hidden_last, preferred_element_type=F32)

    def term(p, xo, part, rows):
        return jnp.dot(adj_t[(p * XS + xo) * 2 + part, rows, :], pulled[...], preferred_element_type=F32)

    class Back:
        def __init__(self, phase, rows):
            self.phase, self.rows = phase, rows
            self.parts = parts_1 if phase else parts_0

        def core_sum(self, q, xo):
            return term(2 * q, xo, self.parts[2 * q], self.rows) + core_in[self.phase, q, xo, self.rows].astype(F32)

        def to_cores(self):
            self.cores = []
            for i in range(2):
                p = 2 * i + 1
                for xo in range(XS):
                    core_out[self.phase, i, xo, self.rows] = term(p, xo, self.parts[p], self.rows).astype(BF16)
                source = core_out.at[self.phase, i, :, self.rows]
                target = core_in.at[self.phase, i + core, :, self.rows]
                self.cores.append(send(source, target, other_core))

        def over(self):
            for copy in self.cores:
                copy.wait_recv()
            self.hops = []
            for i, device in enumerate((prev, next_)):
                zx_out[self.phase, i, self.rows] = self.core_sum(2 * i, xs[2]).astype(BF16)
                target = zx_in.at[self.phase, 1 - i, self.rows]
                self.hops.append(send(zx_out.at[self.phase, i, self.rows], target, device))
            self.x = {}
            for q in (0, 2, 1):
                for j in range(2):
                    self.to_x(q, j, self.core_sum(q, xs[j]))
            for q in range(3):
                own_part[self.phase, q, self.rows] = self.core_sum(q, x)

        def to_x(self, q, j, value):
            x_out[self.phase, q, j, self.rows] = value.astype(BF16)
            source, target = x_out.at[self.phase, q, j, self.rows], x_in.at[self.phase, q, j, self.rows]
            self.x[q, j] = send(source, target, x_devices[j])

        def over_two(self):
            for copy in self.hops:
                copy.wait_recv()
            value = self.core_sum(1, xs[2])
            for i in range(2):
                value = value + zx_in[self.phase, i, self.rows].astype(F32)
            self.to_x(1, 2, value)

        def x_sum(self, q, count):
            total = own_part[self.phase, q, self.rows]
            for j in range(count):
                self.x[q, j].wait_recv()
                total = total + x_in[self.phase, q, j, self.rows].astype(F32)
            return total

        def to_sides(self):
            self.sides = []
            for i, device in enumerate((prev, next_)):
                z_out[self.phase, i, self.rows] = self.x_sum(2 * i, 2).astype(BF16)
                target = z_in.at[self.phase, 1 - i, self.rows]
                self.sides.append(send(z_out.at[self.phase, i, self.rows], target, device))

        def total(self):
            total = self.x_sum(1, 3)
            for copy in self.sides:
                copy.wait_recv()
            for i in range(2):
                total = total + z_in[self.phase, i, self.rows].astype(F32)
            return total

        def to_far(self):
            far_out[self.rows] = self.total().astype(BF16)
            return send(far_out.at[self.rows], far_in.at[self.rows], far)

    first, second, near = Back(1, tiles[0]), Back(1, tiles[1]), Back(0, shard)
    piece_rows = TILE // PLANE
    own_rows = pl.ds(place * piece_rows, piece_rows)

    first.to_cores()
    core_grads.wait_recv()
    grads[core] = grads[core] + grads_core[...]
    plane_grads = [
        send(grads.at[core, pl.ds(to * piece_rows, piece_rows)], grads_plane.at[i], device)
        for i, (to, device) in enumerate(zip(places, plane_devices, strict=True))
    ]
    second.to_cores()
    first.over()
    for copy in plane_grads:
        copy.wait_recv()
    part = grads[core, own_rows]
    for i in range(PLANE - 1):
        part = part + grads_plane[i]
    grads_near[near_slot] = part
    near_grads = [send(grads_near.at[near_slot], grads_near.at[near_slot], device) for device in near_devices]
    second.over()
    first.over_two()
    for copy in near_grads:
        copy.wait_recv()
    part = grads_near[0]
    for i in range(1, NEAR):
        part = part + grads_near[i]
    grads_far[far_slot] = part
    far_grads = [send(grads_far.at[far_slot], grads_far.at[far_slot], device) for device in far_devices]
    second.over_two()
    first.to_sides()
    near.to_cores()
    far_back = [first.to_far()]
    second.to_sides()
    far_back.append(second.to_far())
    near.over()
    near.over_two()
    for copy in far_grads:
        copy.wait_recv()
    factor = 1.0 / math.sqrt(SHARD * lax.axis_size("wide") * lax.axis_size("narrow"))
    piece = grads_all.at[core, own_rows]
    piece[...] = (grads_far[0] + grads_far[1] + grads_far[2] + grads_far[3]) * factor
    plane_grads = [send(piece, piece, device) for device in plane_devices]
    near.to_sides()
    for copy in plane_grads:
        copy.wait_recv()
    core_grads = send(grads_all.at[core], grads_all.at[core], other_core)
    own_total[...] = local_term[...] + near.total()
    for t in range(2):
        far_back[t].wait_recv()
        grad_input[tiles[t]] = (own_total[tiles[t]] + far_in[tiles[t]].astype(F32)).astype(BF16)
    core_grads.wait_recv()
    grad_self[...] = grads_all[0]
    grad_neigh[...] = grads_all[1]
    for copy in sent:
        copy.wait_send()


def body(features, w_self, w_neigh, cotangent, tile_src, tile_live, tile_mask):
    rows, width = features.shape
    hidden = w_self.shape[1]
    slots = tile_src.shape[1]
    vmem = pl.BlockSpec(memory_space=pltpu.VMEM)
    hbm = pl.BlockSpec(memory_space=pl.ANY)
    return pl.pallas_call(
        functools.partial(kernel, slots),
        out_shape=(
            jax.ShapeDtypeStruct((rows, hidden), BF16),
            jax.ShapeDtypeStruct((width, hidden), F32),
            jax.ShapeDtypeStruct((width, hidden), F32),
            jax.ShapeDtypeStruct((rows, width), BF16),
        ),
        in_specs=[hbm] * 7,
        out_specs=[vmem] * 4,
        scratch_shapes=[
            pltpu.VMEM((width, hidden), BF16),
            pltpu.VMEM((width, hidden), BF16),
            pltpu.VMEM((rows, hidden), BF16),
            pltpu.SMEM(tile_src.shape, jnp.int32),
            pltpu.SMEM(tile_live.shape, jnp.int32),
            pltpu.VMEM((2, slots, TILE, TILE), jnp.int32),
            pltpu.VMEM((2 * (slots + 1), TILE, TILE), BF16),
            pltpu.VMEM((2 * (slots + 1), TILE, TILE), BF16),
            pltpu.VMEM((16, TILE), jnp.int32),
            pltpu.SMEM((16, TILE), jnp.int32),
            pltpu.VMEM((SHARDS, SHARD, SHARD), BF16),
            pltpu.VMEM((SHARDS, SHARD, SHARD), BF16),
            pltpu.VMEM((WINDOW, XS, 2, SHARD, TILE), BF16),
            pltpu.VMEM((SHARD, TILE), F32),
            pltpu.VMEM((SHARD, TILE), F32),
            pltpu.VMEM((SHARD, hidden), F32),
            pltpu.VMEM((SHARD, TILE), BF16),
            pltpu.VMEM((SHARD, TILE), BF16),
            pltpu.VMEM((SHARD, TILE), F32),
            pltpu.VMEM((2, 2, XS, SHARD, TILE), BF16),
            pltpu.VMEM((2, 3, XS, SHARD, TILE), BF16),
            pltpu.VMEM((2, 3, 3, SHARD, TILE), BF16),
            pltpu.VMEM((2, 3, 3, SHARD, TILE), BF16),
            pltpu.VMEM((2, 3, SHARD, TILE), F32),
            pltpu.VMEM((2, 2, SHARD, TILE), BF16),
            pltpu.VMEM((2, 2, SHARD, TILE), BF16),
            pltpu.VMEM((2, 2, SHARD, TILE), BF16),
            pltpu.VMEM((2, 2, SHARD, TILE), BF16),
            pltpu.VMEM((SHARD, TILE), F32),
            pltpu.VMEM((SHARD, TILE), BF16),
            pltpu.VMEM((SHARD, TILE), BF16),
            pltpu.VMEM((2, width, hidden), F32),
            pltpu.VMEM((width, hidden), F32),
            pltpu.VMEM((PLANE - 1, width // PLANE, hidden), F32),
            pltpu.VMEM((NEAR, width // PLANE, hidden), F32),
            pltpu.VMEM((FAR, width // PLANE, hidden), F32),
            pltpu.VMEM((2, width, hidden), F32),
            pltpu.SemaphoreType.DMA((TRANSFERS,)),
            pltpu.SemaphoreType.DMA((TRANSFERS,)),
            pltpu.SemaphoreType.DMA((7,)),
            pltpu.SemaphoreType.DMA,
        ],
        compiler_params=pltpu.CompilerParams(
            collective_id=1, has_side_effects=True, vmem_limit_bytes=62 * 1024 * 1024
        ),
    )(features, w_self, w_neigh, cotangent, tile_src, tile_live, tile_mask)


def solution(mesh):
    return jax.shard_map(
        body,
        mesh=mesh,
        in_specs=(
            P(("wide", "narrow"), None),
            P(),
            P(),
            P(("wide", "narrow"), None),
            P(("wide", "narrow"), None),
            P(("wide", "narrow")),
            P(("wide", "narrow"), None, None, None),
        ),
        out_specs=(P(("wide", "narrow"), None), P(), P(), P(("wide", "narrow"), None)),
        check_vma=False,
    )
```

time: 127 us -> 119 us (0.937)
  Pallas kernels: 120 us -> 112 us
    pallas_call x1, Pallas kernels: 120 us -> 112 us  [body(): pl.pallas_call(functools.partial(kernel, slots), out_shape=(jax.ShapeDtyp...]
where the time goes in v2:
time: 119 us; the launch traced here: 118 us
  Pallas kernels  112 us (94%)
  local copies, waits for them, and re-layouts  6.17 us (5%)
    pallas_call x1, Pallas kernels, body(): pl.pallas_call(functools.partial(kernel, slots), out_shape=(jax.ShapeDtyp...  112 us
    unnamed x4, local copies, waits for them, and re-layouts  6.17 us

profile of v2, /device:TPU:1, one launch (start us, length us, event | category | flops | bytes accessed | tf_op | source)
XLA Modules:
  0.0 118.3 jit_solution(2850630419893681092)
XLA Ops:
  0.6 111.5 %shard_map.102 = (bf16[256,256]{1,0:T(8,128)(2,1)}, f32[128,256]{1,0:T(8,128)}, f32[128,256]{1,0:T(8,128)}, bf16[256,128]{1,0:T(8,128)(2,1)}) custom-call(bf16[256,128]{1,0:T(8,128)(2,1)} %features_hbm.1, bf16[128,256]{1,0:T(8,128)(2,1)} %w_self_hbm.1, bf16[128,256]{1,0:T(8,128)(2,1)} %w_neigh_hbm.1, bf16[256,256]{1,0:T(8,128)(2,1)} %cotangent_hbm.1, ...), custom_call_target="tpu_custom_call" | custom-call | tf_op jit(solution)/shard_map/pallas_call | solution.py:461
  112.2 1.6 %copy.15 = bf16[256,256]{1,0:T(8,128)(2,1)} copy(bf16[256,256]{1,0:T(8,128)(2,1)} %get-tuple-element.8) | data formatting | bytes 262144
  113.7 1.6 %copy.16 = f32[128,256]{1,0:T(8,128)} copy(f32[128,256]{1,0:T(8,128)} %get-tuple-element.9) | data formatting | bytes 262144
  115.3 1.6 %copy.17 = f32[128,256]{1,0:T(8,128)} copy(f32[128,256]{1,0:T(8,128)} %get-tuple-element.10) | data formatting | bytes 262144
  116.9 1.5 %copy.18 = bf16[256,128]{1,0:T(8,128)(2,1)} copy(bf16[256,128]{1,0:T(8,128)(2,1)} %get-tuple-element.11) | data formatting | bytes 131072

commit v3 on v2

--- a/solution.py
+++ b/solution.py
@@ -282,14 +282,13 @@
     parts_0, parts_1 = sides(0), sides(1)
     aggregate((0, 2, 4), parts_0)
 
+    to_far[0].wait_recv()
+    to_next_0, to_prev_0, over_x_0, to_core_0 = spread(1, tiles[0])
     to_core.wait_recv()
     side_core.wait_recv()
     for copy in cores_0:
         copy.wait_recv()
     aggregate((1, 3), parts_0)
-
-    to_far[0].wait_recv()
-    to_next_0, to_prev_0, over_x_0, to_core_0 = spread(1, tiles[0])
     over_prev_0, over_next_0, side_core_0 = spread_sides(1, tiles[0], to_next_0, to_prev_0)
     to_far[1].wait_recv()
     to_next_1, to_prev_1, over_x_1, to_core_1 = spread(1, tiles[1])
@@ -307,7 +306,6 @@
     mean_rows[...] = (summed[...] * scaling).astype(BF16)
     preact = pre_self[...] + jnp.dot(mean_rows[...], w_neigh[...], preferred_element_type=F32)
     sigmoid = jax.nn.sigmoid(preact)
-    output[...] = (preact * sigmoid).astype(BF16)
     grad_pre = (cotangent[...].astype(F32) * sigmoid * (1.0 + preact * (1.0 - sigmoid))).astype(BF16)
     rows_first = (((0,), (0,)), ((), ()))
     hidden_last = (((1,), (1,)), ((), ()))
@@ -317,7 +315,6 @@
     pulled[...] = (
         lax.dot_general(grad_pre, w_neigh[...], hidden_last, preferred_element_type=F32) * scaling
     ).astype(BF16)
-    local_term[...] = lax.dot_general(grad_pre, w_self[...], hidden_last, preferred_element_type=F32)
 
     def term(p, xo, part, rows):
         return jnp.dot(adj_t[(p * XS + xo) * 2 + part, rows, :], pulled[...], preferred_element_type=F32)
@@ -406,6 +403,8 @@
         for i, (to, device) in enumerate(zip(places, plane_devices, strict=True))
     ]
     second.to_cores()
+    output[...] = (preact * sigmoid).astype(BF16)
+    local_term[...] = lax.dot_general(grad_pre, w_self[...], hidden_last, preferred_element_type=F32)
     first.over()
     for copy in plane_grads:
         copy.wait_recv()

time: 119 us -> 118 us (level)
  no operation moved by 1% of the time
where the time goes in v3:
time: 118 us
  Pallas kernels  111 us (94%)
  local copies, waits for them, and re-layouts  6.17 us (5%)
    pallas_call x1, Pallas kernels, body(): pl.pallas_call(functools.partial(kernel, slots), out_shape=(jax.ShapeDtyp...  111 us
    unnamed x4, local copies, waits for them, and re-layouts  6.17 us

profile of v3, /device:TPU:1, one launch (start us, length us, event | category | flops | bytes accessed | tf_op | source)
XLA Modules:
  0.0 117.6 jit_solution(11872619468897768952)
XLA Ops:
  0.6 110.7 %shard_map.102 = (bf16[256,256]{1,0:T(8,128)(2,1)}, f32[128,256]{1,0:T(8,128)}, f32[128,256]{1,0:T(8,128)}, bf16[256,128]{1,0:T(8,128)(2,1)}) custom-call(bf16[256,128]{1,0:T(8,128)(2,1)} %features_hbm.1, bf16[128,256]{1,0:T(8,128)(2,1)} %w_self_hbm.1, bf16[128,256]{1,0:T(8,128)(2,1)} %w_neigh_hbm.1, bf16[256,256]{1,0:T(8,128)(2,1)} %cotangent_hbm.1, ...), custom_call_target="tpu_custom_call" | custom-call | tf_op jit(solution)/shard_map/pallas_call | solution.py:460
  111.4 1.6 %copy.15 = bf16[256,256]{1,0:T(8,128)(2,1)} copy(bf16[256,256]{1,0:T(8,128)(2,1)} %get-tuple-element.8) | data formatting | bytes 262144
  112.9 1.6 %copy.16 = f32[128,256]{1,0:T(8,128)} copy(f32[128,256]{1,0:T(8,128)} %get-tuple-element.9) | data formatting | bytes 262144
  114.5 1.6 %copy.17 = f32[128,256]{1,0:T(8,128)} copy(f32[128,256]{1,0:T(8,128)} %get-tuple-element.10) | data formatting | bytes 262144
  116.1 1.5 %copy.18 = bf16[256,128]{1,0:T(8,128)(2,1)} copy(bf16[256,128]{1,0:T(8,128)(2,1)} %get-tuple-element.11) | data formatting | bytes 131072
